TPU v7x, 512 devices: a whole 4x4x16 slice. The times are simulated.
512 devices in a mesh: batch: 256 (over x, z_lo, y, core), mp: 2 (over z_hi).
Axes of the slice: x: 4, y: 4, z: 16 (z_hi: 2, z_lo: 8; z = z_hi * 8 + z_lo), core: 2. Of those that a mesh axis runs over, the one named last changes fastest.
Arguments:
- img_embed: bfloat16 [131072, 1152], P('batch', 'mp'), may hold values from -3 to 3
- txt_embed: bfloat16 [131072, 1152], P('batch', 'mp'), may hold values from -3 to 3
Outputs:
- img_grad: bfloat16 [131072, 1152], P('batch', 'mp')
- txt_grad: bfloat16 [131072, 1152], P('batch', 'mp')
All inputs are finite; a program needn't handle non-finite values.
Results may differ from a plain program's by a relative error of at most 0.0079.
Values may be sent and summed in bfloat16 or wider, within the bound.
A program may use at most 64 MiB of HBM per device.

v0:
```python
import jax
import jax.numpy as jnp
from jax import lax
from jax.sharding import PartitionSpec as P

STEPS = 2


logit_scale = 100.0
logit_bias = -5.0
norm_eps = 1e-06


def shifted(block, axis, distance):
    devices = range(lax.axis_size(axis))
    route = [((i - distance) % len(devices), i) for i in devices]
    return lax.ppermute(block, axis, route)


def contract_rows(left, right):
    return lax.dot_general(
        left, right, (((1,), (1,)), ((), ())), preferred_element_type=jnp.float32
    )


def local(img_embed, txt_embed):
    row_count, half_width = img_embed.shape
    img_values = img_embed.astype(jnp.float32)
    txt_values = txt_embed.astype(jnp.float32)
    img_square, txt_square = lax.psum(
        (jnp.sum(img_values * img_values, axis=1), jnp.sum(txt_values * txt_values, axis=1)), "mp"
    )
    img_inverse = lax.rsqrt(img_square + norm_eps)[:, None]
    txt_inverse = lax.rsqrt(txt_square + norm_eps)[:, None]
    img_unit = img_values * img_inverse
    txt_unit = txt_values * txt_inverse
    img_half = img_unit.astype(jnp.bfloat16)
    txt_half = txt_unit.astype(jnp.bfloat16)
    img_wide, txt_wide = (img_half, txt_half)

    def block_terms(held_block, diagonal):
        scores = lax.psum(contract_rows(img_half, held_block), "mp")
        weights = (jax.nn.sigmoid(logit_scale * scores + logit_bias) - diagonal).astype(
            jnp.bfloat16
        )
        image_part = logit_scale * jnp.dot(weights, held_block, preferred_element_type=jnp.float32)
        caption_part = logit_scale * lax.dot_general(
            weights, img_half, (((0,), (0,)), ((), ())), preferred_element_type=jnp.float32
        )
        return (image_part, caption_part)

    identity = jnp.eye(row_count, dtype=jnp.float32)
    img_total, own_part = block_terms(txt_wide, identity)
    returned = []
    held_block = txt_wide
    for offset in range(1, STEPS + 1):
        held_block = shifted(held_block, "batch", 1)
        image_part, caption_part = block_terms(held_block, jnp.zeros_like(identity))
        img_total = img_total + image_part
        returned.append(caption_part)
    txt_total = own_part
    for offset in range(1, STEPS + 1):
        txt_total = txt_total + shifted(returned[offset - 1], "batch", -offset)
    img_inner, txt_inner = lax.psum(
        (jnp.sum(img_unit * img_total, axis=1), jnp.sum(txt_unit * txt_total, axis=1)), "mp"
    )
    img_grad = (img_total - img_unit * img_inner[:, None]) * img_inverse
    txt_grad = (txt_total - txt_unit * txt_inner[:, None]) * txt_inverse
    return (img_grad.astype(jnp.bfloat16), txt_grad.astype(jnp.bfloat16))


def solution(mesh):
    return jax.shard_map(
        local,
        mesh=mesh,
        in_specs=(P("batch", "mp"), P("batch", "mp")),
        out_specs=(P("batch", "mp"), P("batch", "mp")),
        check_vma=False,
    )
```

profile of v0, /device:TPU:122, one launch (start us, length us, event | category | flops | bytes accessed | tf_op | source)
XLA Modules:
  0.0 460.0 jit_solution(10290008985464695471)
XLA Ops:
  7.2 0.0 copy-start.1
  7.2 0.0 copy-start
  7.2 0.0 all-reduce.5.cloned.1.call-start
  7.2 1.6 fusion.13
  8.8 14.0 %all-reduce.1 = (f32[512]{0:T(512)S(1)}, f32[512]{0:T(512)S(1)}) all-reduce(f32[512]{0:T(512)S(1)} %get-tuple-element.14, f32[512]{0:T(512)S(1)} %get-tuple-element.13), channel_id=1, replica_groups=mesh['batch'=256,'mp'=2] {'mp'}, use_global_device_ids=true, to_apply=%region_3.0 | all-reduce | flops 1024 | bytes 8192 | tf_op jit(solution)/shard_map/psum | solution.py:30
  22.8 0.1 fusion.2
  23.0 1.9 collective-permute-start
  24.9 9.3 %collective-permute-done = bf16[512,576]{0,1:T(8,128)(2,1)S(1)} collective-permute-done((bf16[512,576]{0,1:T(8,128)(2,1)S(1)}, bf16[512,576]{0,1:T(8,128)(2,1)S(1)}, u32[]{:S(2)}, u32[]{:S(2)}) %collective-permute-start) | collective-permute-done | bytes 589856 | tf_op jit(solution)/shard_map/ppermute | solution.py:17
  34.2 2.0 collective-permute-start.1
  36.1 1.6 fusion.26
  37.7 1.6 fusion.24
  39.3 6.0 %collective-permute-done.1 = bf16[512,576]{0,1:T(8,128)(2,1)S(1)} collective-permute-done((bf16[512,576]{0,1:T(8,128)(2,1)S(1)}, bf16[512,576]{0,1:T(8,128)(2,1)S(1)}, u32[]{:S(2)}, u32[]{:S(2)}) %collective-permute-start.1) | collective-permute-done | bytes 589856 | tf_op jit(solution)/shard_map/ppermute | solution.py:17
  45.4 1.6 fusion.22
  47.0 0.0 all-reduce.5.cloned.1.call-update
  47.0 339.9 %all-reduce.5.cloned.1.call-done = (f32[512,512]{1,0:T(8,128)}, f32[512,512]{1,0:T(8,128)}, f32[512,512]{1,0:T(8,128)}) async-done(((f32[512,512]{1,0:T(8,128)}, f32[512,512]{1,0:T(8,128)}, f32[512,512]{1,0:T(8,128)}), (f32[512,512]{1,0:T(8,128)}, f32[512,512]{1,0:T(8,128)}, f32[512,512]{1,0:T(8,128)})) %all-reduce.5.cloned.1.call-update) | async-done | bytes 3145744 | tf_op jit(solution)/shard_map/psum | solution.py:42
  386.9 1.9 convolution_multiply_fusion
  388.8 0.6 convolution_multiply_fusion.1
  389.4 1.9 collective-permute-start.2
  391.3 2.9 collective-permute-start.3
  394.2 0.0 copy-start.6
  394.2 0.6 fusion.28
  394.8 0.5 copy-done.6
  395.3 0.6 convolution_add_fusion.1
  395.9 0.6 copy-done.3
  396.5 0.2 copy-done.8
  396.7 1.3 fusion.9
  397.9 17.9 %collective-permute-done.2 = f32[512,576]{0,1:T(8,128)S(1)} collective-permute-done((f32[512,576]{0,1:T(8,128)S(1)}, f32[512,576]{0,1:T(8,128)S(1)}, u32[]{:S(2)}, u32[]{:S(2)}) %collective-permute-start.2) | collective-permute-done | bytes 1179680 | tf_op jit(solution)/shard_map/ppermute | solution.py:17
  415.9 20.1 %collective-permute-done.3 = f32[512,576]{0,1:T(8,128)S(1)} collective-permute-done((f32[512,576]{0,1:T(8,128)S(1)}, f32[512,576]{0,1:T(8,128)S(1)}, u32[]{:S(2)}, u32[]{:S(2)}) %collective-permute-start.3) | collective-permute-done | bytes 1179680 | tf_op jit(solution)/shard_map/ppermute | solution.py:17
  435.9 1.3 fusion.14
  437.3 13.8 %all-reduce = (f32[512]{0:T(512)S(1)}, f32[512]{0:T(512)S(1)}) all-reduce(f32[512]{0:T(512)} %get-tuple-element.9, f32[512]{0:T(512)} %get-tuple-element.11), channel_id=1, replica_groups=mesh['batch'=256,'mp'=2] {'mp'}, use_global_device_ids=true, to_apply=%region_8.0 | all-reduce | flops 1024 | bytes 8192 | tf_op jit(solution)/shard_map/psum | solution.py:64
  451.0 1.0 fusion.17
  452.1 1.0 fusion.12
  (14 shorter events, 0.0 us)
Async XLA Ops:
  7.2 29.0 %copy-start.1 = (bf16[512,576]{0,1:T(8,128)(2,1)S(1)}, bf16[512,576]{0,1:T(8,128)(2,1)}, u32[]{:S(2)}) copy-start(bf16[512,576]{0,1:T(8,128)(2,1)} %param.2) | copy-start | bytes 1769476
  7.2 15.7 %copy-start = (bf16[512,576]{0,1:T(8,128)(2,1)S(1)}, bf16[512,576]{0,1:T(8,128)(2,1)}, u32[]{:S(2)}) copy-start(bf16[512,576]{0,1:T(8,128)(2,1)} %param.3) | copy-start | bytes 1769476
  7.2 379.7 %all-reduce.5.cloned.1.call-start = ((), (), s32[]{:S(2)}) async-start(), calls=%async_computation | async-start | bytes 6291456 | tf_op jit(solution)/shard_map/psum | solution.py:42
  23.0 11.2 %collective-permute-start = (bf16[512,576]{0,1:T(8,128)(2,1)S(1)}, bf16[512,576]{0,1:T(8,128)(2,1)S(1)}, u32[]{:S(2)}, u32[]{:S(2)}) collective-permute-start(bf16[512,576]{0,1:T(8,128)(2,1)S(1)} %fusion.2), channel_id=1, source_target_pairs={{510,0},{0,2},{2,4},{4,6},{6,8},{8,10},{10,12},{12,14},{14,16},{16... | collective-permute-start | bytes 1769480 | tf_op jit(solution)/shard_map/ppermute | solution.py:17
  34.2 5.2 %copy-start.5 = (bf16[512,576]{0,1:T(8,128)(2,1)}, bf16[512,576]{0,1:T(8,128)(2,1)S(1)}, u32[]{:S(2)}) copy-start(bf16[512,576]{0,1:T(8,128)(2,1)S(1)} %collective-permute-done) | copy-start | bytes 1769476
  34.2 11.2 %collective-permute-start.1 = (bf16[512,576]{0,1:T(8,128)(2,1)S(1)}, bf16[512,576]{0,1:T(8,128)(2,1)S(1)}, u32[]{:S(2)}, u32[]{:S(2)}) collective-permute-start(bf16[512,576]{0,1:T(8,128)(2,1)S(1)} %collective-permute-done), channel_id=1, source_target_pairs={{510,0},{0,2},{2,4},{4,6},{6,8},{8,10},{10,12},{12,14},{14,16},{16... | collective-permute-start | bytes 1769480 | tf_op jit(solution)/shard_map/ppermute | solution.py:17
  45.4 1.7 copy-start.7
  386.9 1.9 copy-start.4
  388.8 5.4 %copy-start.2 = (f32[512,512]{1,0:T(8,128)S(1)}, f32[512,512]{1,0:T(8,128)}, u32[]{:S(2)}) copy-start(f32[512,512]{1,0:T(8,128)} %get-tuple-element.6) | copy-start | bytes 3145732
  389.4 26.5 %collective-permute-start.2 = (f32[512,576]{0,1:T(8,128)S(1)}, f32[512,576]{0,1:T(8,128)S(1)}, u32[]{:S(2)}, u32[]{:S(2)}) collective-permute-start(f32[512,576]{0,1:T(8,128)S(1)} %convolution_multiply_fusion.1), channel_id=1, source_target_pairs={{2,0},{4,2},{6,4},{8,6},{10,8},{12,10},{14,12},{16,14},{18,16},{20... | collective-permute-start | bytes 3538952 | tf_op jit(solution)/shard_map/ppermute | solution.py:17
  391.3 44.6 %collective-permute-start.3 = (f32[512,576]{0,1:T(8,128)S(1)}, f32[512,576]{0,1:T(8,128)S(1)}, u32[]{:S(2)}, u32[]{:S(2)}) collective-permute-start(f32[512,576]{0,1:T(8,128)S(1)} %convolution_multiply_fusion), channel_id=1, source_target_pairs={{4,0},{6,2},{8,4},{10,6},{12,8},{14,10},{16,12},{18,14},{20,16},{2... | collective-permute-start | bytes 3538952 | tf_op jit(solution)/shard_map/ppermute | solution.py:17
  394.2 1.1 copy-start.6
  395.3 1.2 copy-start.3
  395.3 1.4 copy-start.8
Sparse Core Ops, SparseCore 0:
  47.1 339.6 all-reduce.4
where the time goes:
time: 460 us
  waiting for transfers between devices  393 us (85%)
  blocking collectives  27.8 us (6%)
  between operations  14.2 us (3%)
  matrix products  11.1 us (2%)
  starting transfers between devices  8.71 us (2%)
    psum x1, waiting for transfers between devices, block_terms(): scores = lax.psum(contract_rows(img_half, held_block), 'mp')  340 us
    ppermute x4, waiting for transfers between devices, shifted(): return lax.ppermute(block, axis, route)  53.3 us
    psum x1, blocking collectives, local(): lax.psum((jnp.sum(img_values * img_values, axis=1), jnp.sum(txt_values *...  14 us
    psum x1, blocking collectives, local(): lax.psum((jnp.sum(img_unit * img_total, axis=1), jnp.sum(txt_unit * txt_t...  13.8 us
  transfers between devices with their start and end apart: 5, of which 5 were waited for; matrix products, arithmetic and copies ran while one was open for 1% of the time, Pallas kernels for 0%

commit v1 on v0

v1 whole, which is shorter than its diff:
```python
import jax
import jax.numpy as jnp
from jax import lax
from jax.experimental import pallas as pl
from jax.experimental.pallas import tpu as pltpu
from jax.sharding import PartitionSpec as P

MESH = pl.DeviceIdType.MESH
BF16, F32 = jnp.bfloat16, jnp.float32

logit_scale = 100.0
logit_bias = -5.0
norm_eps = 1e-06

ROWS = 512
HALF = 576
MAIN = 512
REST = HALF - MAIN
FULL = 2 * HALF
CHUNK = 32
PACK = CHUNK // 2
STEPS = ROWS // 2 // CHUNK
ALL = 2 * STEPS
AHEAD = 3
LAND, RELAY, CHIP, CALC = 1, 2, 4, 5
LEG1, LEG2, HALO, VIA, PAIR = range(5)


def nt(left, right):
    return lax.dot_general(left, right, (((1,), (1,)), ((), ())), preferred_element_type=F32)


def weigh(scores):
    return 1.0 / (1.0 + jnp.exp(-(logit_scale * scores + logit_bias)))


def kernel(img_ref, txt_ref, img_out, txt_out, stage, land, full, inverse, txt_main, txt_rest, txt_inner, sent, came):
    batch, side = lax.axis_index("batch"), lax.axis_index("mp")
    core = lax.rem(batch, 2)
    y = lax.rem(lax.div(batch, 2), 4)
    z_lo = lax.rem(lax.div(batch, 8), 8)
    x = lax.div(batch, 64)
    z = side * 8 + z_lo

    def device(x, y, z, core):
        x, y, z = lax.rem(x + 4, 4), lax.rem(y + 4, 4), lax.rem(z + 16, 16)
        return (((x * 8 + lax.rem(z, 8)) * 4 + y) * 2 + core, lax.div(z, 8))

    def along_z(distance):
        return device(x, y, z + distance, core)

    x_next = x + lax.div(z_lo, 7)
    x_before = x - 1 + lax.div(z_lo + 7, 8)

    barrier = pltpu.get_barrier_semaphore()

    def greet(where):
        pl.semaphore_signal(barrier, inc=1, device_id=where, device_id_type=MESH)

    for distance in (1, -1, 7, -7):
        greet(along_z(distance))
    greet(device(x, y, z, 1 - core))
    for distance in (1, 2, 3):
        greet(device(x, y + distance, z, core))

    @pl.when(y == 0)
    def _():
        for column in range(4):
            greet(device(x_before, column, z - 1, core))

    @pl.when(y == 3)
    def _():
        for column in range(4):
            greet(device(x_next, column, z + 1, core))

    lane = lax.broadcasted_iota(jnp.int32, (PACK, 2 * REST), 1)

    def pack(ref, array):
        def one(chunk, carry):
            row = pl.multiple_of(chunk * CHUNK, CHUNK)
            low = ref[pl.ds(row, PACK), :]
            high = ref[pl.ds(row + PACK, PACK), :]
            stage[array, chunk, :, :MAIN] = low[:, :MAIN]
            stage[array, chunk, :, MAIN : 2 * MAIN] = high[:, :MAIN]
            stage[array, chunk, :, 2 * MAIN :] = jnp.concatenate([low[:, MAIN:], high[:, MAIN:]], axis=1)
            return carry

        lax.fori_loop(0, 2 * STEPS, one, 0)

    pack(txt_ref, 0)
    pack(img_ref, 1)
    txt_main[...] = jnp.zeros_like(txt_main)
    txt_rest[...] = jnp.zeros_like(txt_rest)
    txt_inner[...] = jnp.zeros_like(txt_inner)
    pl.semaphore_wait(barrier, 10)

    def split(t):
        return lax.div(t, STEPS), lax.rem(t, STEPS)

    def copy(kind, t, way, source, target, where):
        return pltpu.make_async_remote_copy(
            src_ref=source,
            dst_ref=target,
            send_sem=sent.at[kind, t, way],
            recv_sem=came.at[kind, t, way],
            device_id=where,
            device_id_type=MESH,
        )

    def first_leg(t, way):
        array, step = split(t)
        chunk = way * STEPS + step
        return copy(LEG1, t, way, stage.at[array, chunk], land.at[0, array, chunk], along_z(7 - 14 * way))

    def second_leg(t, way):
        array, step = split(t)
        chunk = way * STEPS + step
        return copy(LEG2, t, way, land.at[0, array, chunk], land.at[1, array, chunk], along_z(1 - 2 * way))

    def rows_of(t, way):
        array, step = split(t)
        return pl.ds(pl.multiple_of(way * (ROWS // 2) + step * CHUNK, CHUNK), CHUNK)

    def mirror(array, column):
        return column + array * (3 - 2 * column)

    def via_column(t, way):
        array, step = split(t)
        return lax.rem(2 * step + way, 4)

    def edge(array):
        return device(x_next + array * (x_before - x_next), 3 * array, z + 1 - 2 * array, core)

    def halo(t, way, where, source, target, kind):
        array, step = split(t)
        rows = rows_of(t, way)
        return copy(kind, t, way, full.at[source, rows], full.at[target, rows], where)

    def halo_start(t, way):
        array, step = split(t)
        own, next_one = 3 * array, 3 * array + 2
        place = mirror(array, y)
        via = via_column(t, way)

        @pl.when(place < 3)
        def _():
            halo(t, way, device(x, y + 1 - 2 * array, z, core), own, next_one, HALO).start()

        @pl.when(jnp.logical_and(place == 3, via == 3))
        def _():
            halo(t, way, edge(array), own, next_one, HALO).start()

        @pl.when(jnp.logical_and(place == 3, via < 3))
        def _():
            rows = rows_of(t, way)
            pltpu.make_async_remote_copy(
                src_ref=full.at[own, rows],
                dst_ref=full.at[6 + array, rows],
                send_sem=sent.at[HALO, t, way],
                recv_sem=came.at[VIA, t, way],
                device_id=device(x, mirror(array, via), z, core),
                device_id_type=MESH,
            ).start()

    def on_relay(t, way):
        array, step = split(t)
        via = via_column(t, way)
        return jnp.logical_and(mirror(array, y) == via, via < 3)

    def relay_copy(t, way):
        array, step = split(t)
        rows = rows_of(t, way)
        return pltpu.make_async_remote_copy(
            src_ref=full.at[6 + array, rows],
            dst_ref=full.at[3 * array + 2, rows],
            send_sem=sent.at[VIA, t, way],
            recv_sem=came.at[HALO, t, way],
            device_id=edge(array),
            device_id_type=MESH,
        )

    def pair_copy(t, way):
        array, step = split(t)
        source = 3 * array + 2 * (core + array * (1 - 2 * core))
        return halo(t, way, device(x, y, z, 1 - core), source, 3 * array + 1, PAIR)

    def arrive(t, way):
        array, step = split(t)
        chunk = way * STEPS + step
        row = pl.multiple_of(way * (ROWS // 2) + step * CHUNK, CHUNK)
        mine = stage[array, chunk].astype(F32)
        other = land[1, array, chunk].astype(F32)
        square = mine * mine + other * other
        rest_square = square[:, 2 * MAIN :]
        first = jnp.where(side == 0, mine[:, 2 * MAIN :], other[:, 2 * MAIN :])
        second = jnp.where(side == 0, other[:, 2 * MAIN :], mine[:, 2 * MAIN :])
        for part in range(2):
            total = jnp.sum(square[:, part * MAIN : (part + 1) * MAIN], axis=1, keepdims=True)
            inside = (lane < REST) if part == 0 else (lane >= REST)
            total = total + jnp.sum(jnp.where(inside, rest_square, 0.0), axis=1, keepdims=True)
            scale = lax.rsqrt(total + norm_eps)
            rows = pl.ds(pl.multiple_of(row + part * PACK, PACK), PACK)
            inverse[array, rows, :] = jnp.broadcast_to(scale, (PACK, 128))
            own = 3 * array
            mine_at = pl.ds(pl.multiple_of(side * MAIN, MAIN), MAIN)
            other_at = pl.ds(pl.multiple_of((1 - side) * MAIN, MAIN), MAIN)
            columns = slice(part * MAIN, (part + 1) * MAIN)
            full[own, rows, mine_at] = (mine[:, columns] * scale).astype(BF16)
            full[own, rows, other_at] = (other[:, columns] * scale).astype(BF16)
            if part == 0:
                rest = jnp.where(lane < REST, first, pltpu.roll(second, REST, 1))
            else:
                rest = jnp.where(lane < REST, pltpu.roll(first, REST, 1), second)
            full[own, rows, 2 * MAIN :] = (rest * scale).astype(BF16)

    main_at = pl.ds(pl.multiple_of(side * MAIN, MAIN), MAIN)

    def own_rest(rest):
        return jnp.where(side == 0, rest, pltpu.roll(rest, REST, 1))[:, :REST]

    def finish(ref, out, array, rows, main, rest, inner):
        scale = inverse[array, rows, :][:, :1]
        inner = logit_scale * inner
        values = ref[rows, :].astype(F32)
        unit = values[:, :MAIN] * scale
        out[rows, :MAIN] = ((logit_scale * main - unit * inner) * scale).astype(BF16)
        unit = values[:, MAIN:] * scale
        out[rows, MAIN:] = ((logit_scale * own_rest(rest) - unit * inner) * scale).astype(BF16)

    def images(t):
        both = [rows_of(t, way) for way in range(2)]
        array, step = split(t)
        block = jnp.concatenate([full[3, rows, :] for rows in both], axis=0)
        shape = (2 * CHUNK, ROWS)
        row = lax.broadcasted_iota(jnp.int32, shape, 0)
        row = row + step * CHUNK + jnp.where(row < CHUNK, 0, ROWS // 2 - CHUNK)
        matching = row == lax.broadcasted_iota(jnp.int32, shape, 1)
        main = jnp.zeros((2 * CHUNK, MAIN), F32)
        rest = jnp.zeros((2 * CHUNK, 2 * REST), F32)
        inner = jnp.zeros((2 * CHUNK, 1), F32)
        for offset in range(3):
            scores = nt(block, full[offset])
            weights = weigh(scores)
            if offset == 0:
                weights = jnp.where(matching, weights - 1.0, weights)
            inner = inner + jnp.sum(weights * scores, axis=1, keepdims=True)
            weights = weights.astype(BF16)
            main = main + jnp.dot(weights, full[offset, :, main_at], preferred_element_type=F32)
            rest = rest + jnp.dot(weights, full[offset, :, 2 * MAIN :], preferred_element_type=F32)
        for way, rows in enumerate(both):
            part = slice(way * CHUNK, (way + 1) * CHUNK)
            finish(img_ref, img_out, 1, rows, main[part], rest[part], inner[part])

    def captions(t):
        both = [rows_of(t, way) for way in range(2)]
        array, step = split(t)
        wide = 6 * CHUNK
        block = jnp.concatenate([full[3 + offset, rows, :] for offset in range(3) for rows in both], axis=0)
        block_main = jnp.concatenate([full[3 + offset, rows, main_at] for offset in range(3) for rows in both], axis=0)
        shape = (ROWS, wide)
        column = lax.broadcasted_iota(jnp.int32, shape, 1)
        place = column + step * CHUNK + jnp.where(column < CHUNK, 0, ROWS // 2 - CHUNK)
        matching = jnp.logical_and(column < 2 * CHUNK, place == lax.broadcasted_iota(jnp.int32, shape, 0))
        scores = nt(full[0], block)
        weights = weigh(scores)
        weights = jnp.where(matching, weights - 1.0, weights)
        txt_inner[...] += weights * scores
        weights = weights.astype(BF16)
        txt_main[...] += jnp.dot(weights, block_main, preferred_element_type=F32)
        txt_rest[...] += jnp.dot(weights, block[:, 2 * MAIN :], preferred_element_type=F32)

    for t in range(AHEAD):
        for way in range(2):
            first_leg(t, way).start()

    def during(t, body):
        @pl.when(jnp.logical_and(t >= 0, t < ALL))
        def _():
            for way in range(2):
                body(t, way)

    def step(now, carry):
        during(now + AHEAD, lambda t, way: first_leg(t, way).start())

        def pass_on(t, way):
            first_leg(t, way).wait_recv()
            second_leg(t, way).start()

        during(now, pass_on)

        def take(t, way):
            second_leg(t, way).wait_recv()
            arrive(t, way)
            halo_start(t, way)

        during(now - LAND, take)

        def relay(t, way):
            @pl.when(on_relay(t, way))
            def _():
                array, _ = split(t)
                rows = rows_of(t, way)
                halo(t, way, along_z(1), 6 + array, 6 + array, VIA).wait_recv()
                relay_copy(t, way).start()

        during(now - RELAY, relay)

        def to_pair(t, way):
            array, _ = split(t)
            halo(t, way, along_z(1), 3 * array, 3 * array + 2, HALO).wait_recv()
            pair_copy(t, way).start()

        during(now - CHIP, to_pair)

        t = now - CALC

        @pl.when(jnp.logical_and(t >= STEPS, t < ALL))
        def _():
            images(t)

        during(t, lambda t, way: pair_copy(t, way).wait_recv())

        @pl.when(jnp.logical_and(t >= STEPS, t < ALL))
        def _():
            captions(t)

        return carry

    lax.fori_loop(0, ALL + CALC, step, 0)

    def last(block, carry):
        rows = pl.ds(pl.multiple_of(block * 64, 64), 64)
        inner = jnp.sum(txt_inner[rows, :], axis=1, keepdims=True)
        finish(txt_ref, txt_out, 0, rows, txt_main[rows, :], txt_rest[rows, :], inner)
        return carry

    lax.fori_loop(0, ROWS // 64, last, 0)

    def drain(t, carry):
        array, _ = split(t)
        for way in range(2):
            first_leg(t, way).wait_send()
            second_leg(t, way).wait_send()
            halo(t, way, along_z(1), 3 * array, 3 * array + 2, HALO).wait_send()
            pair_copy(t, way).wait_send()

            @pl.when(on_relay(t, way))
            def _():
                relay_copy(t, way).wait_send()

        return carry

    lax.fori_loop(0, ALL, drain, 0)


def local(img_embed, txt_embed):
    vmem = pl.BlockSpec(memory_space=pltpu.VMEM)
    return pl.pallas_call(
        kernel,
        out_shape=(jax.ShapeDtypeStruct((ROWS, HALF), BF16),) * 2,
        in_specs=[vmem, vmem],
        out_specs=(vmem, vmem),
        scratch_shapes=[
            pltpu.VMEM((2, 2 * STEPS, PACK, FULL), BF16),
            pltpu.VMEM((2, 2, 2 * STEPS, PACK, FULL), BF16),
            pltpu.VMEM((8, ROWS, FULL), BF16),
            pltpu.VMEM((2, ROWS, 128), F32),
            pltpu.VMEM((ROWS, MAIN), F32),
            pltpu.VMEM((ROWS, 2 * REST), F32),
            pltpu.VMEM((ROWS, 6 * CHUNK), F32),
            pltpu.SemaphoreType.DMA((5, ALL, 2)),
            pltpu.SemaphoreType.DMA((5, ALL, 2)),
        ],
        compiler_params=pltpu.CompilerParams(
            collective_id=0, has_side_effects=True, vmem_limit_bytes=48 * 2**20
        ),
        name="gather_and_grad",
    )(img_embed, txt_embed)


def solution(mesh):
    return jax.shard_map(
        local,
        mesh=mesh,
        in_specs=(P("batch", "mp"), P("batch", "mp")),
        out_specs=(P("batch", "mp"), P("batch", "mp")),
        check_vma=False,
    )
```

time: 460 us -> 156 us (0.34)
  the two profiles are of different devices: /device:TPU:122 before, /device:TPU:25 now
where the time goes in v1:
time: 156 us; the launch traced here: 155 us
  Pallas kernels  150 us (96%)
  local copies, waits for them, and re-layouts  3.83 us (2%)
    pallas_call x1, Pallas kernels, local(): pl.pallas_call(kernel, out_shape=(jax.ShapeDtypeStruct((ROWS, HALF), BF16...  150 us

profile of v1, /device:TPU:25, one launch (start us, length us, event | category | flops | bytes accessed | tf_op | source)
XLA Modules:
  0.0 154.7 jit_solution(9394194877670313481)
XLA Ops:
  0.6 0.0 copy-start
  0.6 1.4 copy.4.img_ref
  2.1 0.0 copy-done
  2.1 0.3 copy.5.txt_ref
  2.4 150.2 %gather_and_grad.1 = (bf16[512,576]{1,0:T(8,128)(2,1)S(1)}, bf16[512,576]{1,0:T(8,128)(2,1)S(1)}) custom-call(bf16[512,576]{1,0:T(8,128)(2,1)S(1)} %copy.4.img_ref, bf16[512,576]{1,0:T(8,128)(2,1)S(1)} %copy.5.txt_ref), custom_call_target="tpu_custom_call" | custom-call | tf_op jit(solution)/shard_map/gather_and_grad/pallas_call | solution.py:358
  152.5 1.1 copy.6
  153.6 1.1 copy.7
Async XLA Ops:
  0.6 1.4 copy-start

commit v2 on v1

--- a/solution.py
+++ b/solution.py
@@ -22,7 +22,7 @@
 STEPS = ROWS // 2 // CHUNK
 ALL = 2 * STEPS
 AHEAD = 3
-LAND, RELAY, CHIP, CALC = 1, 2, 4, 5
+LAND, RELAY, CHIP, CALC = 1, 2, 3, 4
 LEG1, LEG2, HALO, VIA, PAIR = range(5)
 
 
@@ -34,7 +34,10 @@
     return 1.0 / (1.0 + jnp.exp(-(logit_scale * scores + logit_bias)))
 
 
-def kernel(img_ref, txt_ref, img_out, txt_out, stage, land, full, inverse, txt_main, txt_rest, txt_inner, sent, came):
+def kernel(
+    img_hbm, txt_hbm, img_out, txt_out, img_ref, txt_ref, stage, land, full, inverse, txt_main, txt_rest, txt_inner,
+    sent, came, load,
+):
     batch, side = lax.axis_index("batch"), lax.axis_index("mp")
     core = lax.rem(batch, 2)
     y = lax.rem(lax.div(batch, 2), 4)
@@ -74,6 +77,11 @@
             greet(device(x_next, column, z + 1, core))
 
     lane = lax.broadcasted_iota(jnp.int32, (PACK, 2 * REST), 1)
+
+    txt_load = pltpu.make_async_copy(txt_hbm, txt_ref, load.at[0])
+    img_load = pltpu.make_async_copy(img_hbm, img_ref, load.at[1])
+    txt_load.start()
+    img_load.start()
 
     def pack(ref, array):
         def one(chunk, carry):
@@ -87,11 +95,8 @@
 
         lax.fori_loop(0, 2 * STEPS, one, 0)
 
+    txt_load.wait()
     pack(txt_ref, 0)
-    pack(img_ref, 1)
-    txt_main[...] = jnp.zeros_like(txt_main)
-    txt_rest[...] = jnp.zeros_like(txt_rest)
-    txt_inner[...] = jnp.zeros_like(txt_inner)
     pl.semaphore_wait(barrier, 10)
 
     def split(t):
@@ -126,7 +131,8 @@
 
     def via_column(t, way):
         array, step = split(t)
-        return lax.rem(2 * step + way, 4)
+        via = lax.rem(2 * step + way, 4)
+        return via + array * lax.div(step, STEPS - 1) * (3 - via)
 
     def edge(array):
         return device(x_next + array * (x_before - x_next), 3 * array, z + 1 - 2 * array, core)
@@ -273,6 +279,12 @@
         for way in range(2):
             first_leg(t, way).start()
 
+    img_load.wait()
+    pack(img_ref, 1)
+    txt_main[...] = jnp.zeros_like(txt_main)
+    txt_rest[...] = jnp.zeros_like(txt_rest)
+    txt_inner[...] = jnp.zeros_like(txt_inner)
+
     def during(t, body):
         @pl.when(jnp.logical_and(t >= 0, t < ALL))
         def _():
@@ -280,13 +292,12 @@
                 body(t, way)
 
     def step(now, carry):
-        during(now + AHEAD, lambda t, way: first_leg(t, way).start())
-
         def pass_on(t, way):
             first_leg(t, way).wait_recv()
             second_leg(t, way).start()
 
         during(now, pass_on)
+        during(now + AHEAD, lambda t, way: first_leg(t, way).start())
 
         def take(t, way):
             second_leg(t, way).wait_recv()
@@ -312,17 +323,18 @@
 
         during(now - CHIP, to_pair)
 
-        t = now - CALC
-
-        @pl.when(jnp.logical_and(t >= STEPS, t < ALL))
-        def _():
-            images(t)
-
-        during(t, lambda t, way: pair_copy(t, way).wait_recv())
-
-        @pl.when(jnp.logical_and(t >= STEPS, t < ALL))
-        def _():
-            captions(t)
+        during(now - CALC, lambda t, way: pair_copy(t, way).wait_recv())
+        before = now - CALC
+
+        @pl.when(jnp.logical_and(before >= STEPS, before < ALL))
+        def _():
+            captions(before)
+
+        before_pair = now - CHIP
+
+        @pl.when(jnp.logical_and(before_pair >= STEPS, before_pair < ALL))
+        def _():
+            images(before_pair)
 
         return carry
 
@@ -358,9 +370,11 @@
     return pl.pallas_call(
         kernel,
         out_shape=(jax.ShapeDtypeStruct((ROWS, HALF), BF16),) * 2,
-        in_specs=[vmem, vmem],
+        in_specs=[pl.BlockSpec(memory_space=pl.ANY)] * 2,
         out_specs=(vmem, vmem),
         scratch_shapes=[
+            pltpu.VMEM((ROWS, HALF), BF16),
+            pltpu.VMEM((ROWS, HALF), BF16),
             pltpu.VMEM((2, 2 * STEPS, PACK, FULL), BF16),
             pltpu.VMEM((2, 2, 2 * STEPS, PACK, FULL), BF16),
             pltpu.VMEM((8, ROWS, FULL), BF16),
@@ -370,6 +384,7 @@
             pltpu.VMEM((ROWS, 6 * CHUNK), F32),
             pltpu.SemaphoreType.DMA((5, ALL, 2)),
             pltpu.SemaphoreType.DMA((5, ALL, 2)),
+            pltpu.SemaphoreType.DMA((2,)),
         ],
         compiler_params=pltpu.CompilerParams(
             collective_id=0, has_side_effects=True, vmem_limit_bytes=48 * 2**20

time: 156 us -> 151 us (0.968)
  Pallas kernels: 150 us -> 146 us
    pallas_call x1, Pallas kernels: 150 us -> 146 us  [local(): pl.pallas_call(kernel, out_shape=(jax.ShapeDtypeStruct((ROWS, HALF), BF16...]
where the time goes in v2:
time: 151 us; the launch traced here: 150 us
  Pallas kernels  146 us (97%)
  local copies, waits for them, and re-layouts  3.83 us (3%)
    pallas_call x1, Pallas kernels, local(): pl.pallas_call(kernel, out_shape=(jax.ShapeDtypeStruct((ROWS, HALF), BF16...  146 us

profile of v2, /device:TPU:25, one launch (start us, length us, event | category | flops | bytes accessed | tf_op | source)
XLA Modules:
  0.0 150.1 jit_solution(5762395125851080879)
XLA Ops:
  0.6 0.0 copy-start
  0.6 1.4 copy.4.img_hbm
  2.1 0.0 copy-done
  2.1 0.3 copy.5.txt_hbm
  2.4 145.6 %gather_and_grad.1 = (bf16[512,576]{1,0:T(8,128)(2,1)S(1)}, bf16[512,576]{1,0:T(8,128)(2,1)S(1)}) custom-call(bf16[512,576]{1,0:T(8,128)(2,1)S(1)} %copy.4.img_hbm, bf16[512,576]{1,0:T(8,128)(2,1)S(1)} %copy.5.txt_hbm), custom_call_target="tpu_custom_call" | custom-call | tf_op jit(solution)/shard_map/gather_and_grad/pallas_call | solution.py:370
  148.0 1.1 copy.6
  149.1 1.1 copy.7
Async XLA Ops:
  0.6 1.4 copy-start

commit v3 on v2

--- a/solution.py
+++ b/solution.py
@@ -131,8 +131,10 @@
 
     def via_column(t, way):
         array, step = split(t)
-        via = lax.rem(2 * step + way, 4)
-        return via + array * lax.div(step, STEPS - 1) * (3 - via)
+        spread = lax.rem(2 * step + way, 4)
+        late = lax.div(step, STEPS - 2)
+        others = lax.rem(2 * step + way, 3)
+        return spread + array * (others + late * (3 - others) - spread)
 
     def edge(array):
         return device(x_next + array * (x_before - x_next), 3 * array, z + 1 - 2 * array, core)
@@ -291,6 +293,10 @@
             for way in range(2):
                 body(t, way)
 
+    def done_before(now):
+        level = lax.div(now, ALL - 1)
+        return (2 * now - ALL + 1) * (1 - level) + (now - 1) * level
+
     def step(now, carry):
         def pass_on(t, way):
             first_leg(t, way).wait_recv()
@@ -322,7 +328,6 @@
             pair_copy(t, way).start()
 
         during(now - CHIP, to_pair)
-
         during(now - CALC, lambda t, way: pair_copy(t, way).wait_recv())
         before = now - CALC
 
@@ -330,11 +335,16 @@
         def _():
             captions(before)
 
-        before_pair = now - CHIP
-
-        @pl.when(jnp.logical_and(before_pair >= STEPS, before_pair < ALL))
-        def _():
-            images(before_pair)
+        @pl.when(jnp.logical_and(now >= STEPS + CHIP, now <= ALL))
+        def _():
+            def rows(t, carry):
+                @pl.when(t >= STEPS)
+                def _():
+                    images(t)
+
+                return carry
+
+            lax.fori_loop(done_before(now), done_before(now + 1), rows, 0)
 
         return carry
 

time: 151 us -> 151 us (level)
  no operation moved by 1% of the time
where the time goes in v3:
time: 151 us
  Pallas kernels  146 us (97%)
  local copies, waits for them, and re-layouts  3.83 us (3%)
    pallas_call x1, Pallas kernels, local(): pl.pallas_call(kernel, out_shape=(jax.ShapeDtypeStruct((ROWS, HALF), BF16...  146 us

profile of v3, /device:TPU:25, one launch (start us, length us, event | category | flops | bytes accessed | tf_op | source)
XLA Modules:
  0.0 150.6 jit_solution(11638389798149211010)
XLA Ops:
  0.6 0.0 copy-start
  0.6 1.4 copy.4.img_hbm
  2.1 0.0 copy-done
  2.1 0.3 copy.5.txt_hbm
  2.4 146.1 %gather_and_grad.1 = (bf16[512,576]{1,0:T(8,128)(2,1)S(1)}, bf16[512,576]{1,0:T(8,128)(2,1)S(1)}) custom-call(bf16[512,576]{1,0:T(8,128)(2,1)S(1)} %copy.4.img_hbm, bf16[512,576]{1,0:T(8,128)(2,1)S(1)} %copy.5.txt_hbm), custom_call_target="tpu_custom_call" | custom-call | tf_op jit(solution)/shard_map/gather_and_grad/pallas_call | solution.py:380
  148.5 1.1 copy.6
  149.6 1.1 copy.7
Async XLA Ops:
  0.6 1.4 copy-start

commit v4 on v3

--- a/solution.py
+++ b/solution.py
@@ -303,7 +303,6 @@
             second_leg(t, way).start()
 
         during(now, pass_on)
-        during(now + AHEAD, lambda t, way: first_leg(t, way).start())
 
         def take(t, way):
             second_leg(t, way).wait_recv()
@@ -321,6 +320,7 @@
                 relay_copy(t, way).start()
 
         during(now - RELAY, relay)
+        during(now + AHEAD, lambda t, way: first_leg(t, way).start())
 
         def to_pair(t, way):
             array, _ = split(t)

time: 151 us -> 151 us (level)
  no operation moved by 1% of the time
where the time goes in v4:
time: 151 us
  Pallas kernels  146 us (97%)
  local copies, waits for them, and re-layouts  3.83 us (3%)
    pallas_call x1, Pallas kernels, local(): pl.pallas_call(kernel, out_shape=(jax.ShapeDtypeStruct((ROWS, HALF), BF16...  146 us

profile of v4, /device:TPU:25, one launch (start us, length us, event | category | flops | bytes accessed | tf_op | source)
XLA Modules:
  0.0 150.5 jit_solution(2445913691552172325)
XLA Ops:
  0.6 0.0 copy-start
  0.6 1.4 copy.4.img_hbm
  2.1 0.0 copy-done
  2.1 0.3 copy.5.txt_hbm
  2.4 146.0 %gather_and_grad.1 = (bf16[512,576]{1,0:T(8,128)(2,1)S(1)}, bf16[512,576]{1,0:T(8,128)(2,1)S(1)}) custom-call(bf16[512,576]{1,0:T(8,128)(2,1)S(1)} %copy.4.img_hbm, bf16[512,576]{1,0:T(8,128)(2,1)S(1)} %copy.5.txt_hbm), custom_call_target="tpu_custom_call" | custom-call | tf_op jit(solution)/shard_map/gather_and_grad/pallas_call | solution.py:380
  148.4 1.1 copy.6
  149.5 1.1 copy.7
Async XLA Ops:
  0.6 1.4 copy-start
